TPU v7x, 512 devices: a whole 4x8x8 slice. The times are simulated.
512 devices in a mesh: row: 16 (over z, core), col: 32 (over y, x).
Axes of the slice: x: 4, y: 8, z: 8, core: 2. Of those that a mesh axis runs over, the one named last changes fastest.
Arguments:
- src_points: float32 [50, 32768], P(None, ('row', 'col')), may hold values from -25 to 25
- dst_points: float32 [50, 98304], P(None, ('col', 'row')), may hold values from -25 to 25
- log_a: float32 [32768], P('row'), may hold values from -1 to 1
- log_b: float32 [98304], P('col'), may hold values from -1 to 1
- dst_potential: float32 [98304], P('col'), may hold values from -6 to 60
Outputs:
- src_potential: float32 [32768], P('row')
- new_potential: float32 [98304], P('col')
All inputs are finite; a program needn't handle non-finite values.
Results may differ from a plain program's by a relative error of at most 0.00013.
Values sent between devices are 32-bit elements; how exact they have to be, the bound alone decides.
No kernel may reach another device: no remote copies, remote signals or barrier semaphores. Data moves between devices by JAX's collectives and lax.ppermute only.
A program may use at most 64 MiB of HBM per device.

v0:
```python
import jax
import jax.numpy as jnp
from jax import lax
from jax.sharding import PartitionSpec as P

epsilon = 0.5


def joined(part, axis, combine):
    gathered = jax.tree.map(lambda a: lax.all_gather(a, axis), part)

    def take(source):
        return jax.tree.map(lambda a: lax.dynamic_index_in_dim(a, source, 0, False), gathered)

    return lax.fori_loop(
        1, lax.axis_size(axis), lambda source, state: combine(state, take(source)), take(0)
    )


def cost_rows(points_block, norms_block, targets, target_norms):
    inner = lax.dot_general(
        points_block,
        targets,
        (((0,), (0,)), ((), ())),
        precision=lax.Precision.HIGHEST,
        preferred_element_type=jnp.float32,
    )
    return norms_block[:, None] + target_norms[None, :] - 2.0 * inner


def combine_lse(first, second):
    highest = jnp.maximum(first[0], second[0])
    return (
        highest,
        first[1] * jnp.exp(first[0] - highest) + second[1] * jnp.exp(second[0] - highest),
    )


def local(src_points, dst_points, log_a, log_b, dst_potential):
    sources = lax.all_gather(src_points, "col", axis=1, tiled=True)
    targets = lax.all_gather(dst_points, "row", axis=1, tiled=True)
    src_norms = jnp.sum(sources * sources, 0)
    dst_norms = jnp.sum(targets * targets, 0)
    width = sources.shape[0]
    rows = sources.shape[1]
    block_rows = 512
    blocks = rows // block_rows
    src_blocks = sources.reshape(width, blocks, block_rows).transpose(1, 0, 2)
    norm_blocks = src_norms.reshape(blocks, block_rows)

    def row_scores(points_block, norms_block):
        return (
            dst_potential[None, :] - cost_rows(points_block, norms_block, targets, dst_norms)
        ) / epsilon

    def local_high(operands):
        return jnp.max(row_scores(operands[0], operands[1]), 1)

    highs = lax.map(local_high, (src_blocks, norm_blocks))
    row_high = lax.pmax(highs.reshape(rows), "col")

    def local_total(operands):
        scores = row_scores(operands[0], operands[1])
        return jnp.sum(jnp.exp(scores - operands[2][:, None]), 1)

    totals = lax.map(local_total, (src_blocks, norm_blocks, row_high.reshape(blocks, block_rows)))
    row_total = lax.psum(totals.reshape(rows), "col")
    src_potential = epsilon * log_a - epsilon * (row_high + jnp.log(row_total))
    potential_blocks = src_potential.reshape(blocks, block_rows)

    def advance(running, operands):
        points_block, norms_block, potential_block = operands
        scores = (
            potential_block[:, None] - cost_rows(points_block, norms_block, targets, dst_norms)
        ) / epsilon
        highest = jnp.max(scores, 0)
        summed = jnp.sum(jnp.exp(scores - highest[None, :]), 0)
        return (combine_lse(running, (highest, summed)), None)

    initial = (
        jnp.full(dst_norms.shape, -jnp.inf, jnp.float32),
        jnp.zeros(dst_norms.shape, jnp.float32),
    )
    (col_high, col_total), unused = lax.scan(
        advance, initial, (src_blocks, norm_blocks, potential_blocks)
    )
    final_high, final_total = joined((col_high, col_total), "row", combine_lse)
    new_potential = epsilon * log_b - epsilon * (final_high + jnp.log(final_total))
    return (src_potential, new_potential)


def solution(mesh):
    return jax.shard_map(
        local,
        mesh=mesh,
        in_specs=(P(None, ("row", "col")), P(None, ("col", "row")), P("row"), P("col"), P("col")),
        out_specs=(P("row"), P("col")),
        check_vma=False,
    )
```

profile of v0, /device:TPU:1, one launch (start us, length us, event | category | flops | bytes accessed | tf_op | source)
XLA Modules:
  0.0 344.4 jit_solution(4888025780347508930)
XLA Ops:
  0.6 0.0 copy-start.3
  0.6 40.1 %all-gather.2 = f32[32,64,50]{1,2,0:T(8,128)S(1)} all-gather(f32[1,64,50]{1,2,0:T(8,128)} %bitcast.89), channel_id=1, replica_groups=mesh['row'=16,'col'=32] {'col'}, dimensions={0}, use_global_device_ids=true | all-gather | bytes 422400 | tf_op jit(solution)/shard_map/all_gather | solution.py:40
  40.8 0.2 copy.17
  40.9 0.3 reshape.51
  41.3 0.3 reshape.39
  41.5 0.1 copy.19
  41.7 38.0 %all-gather.3 = f32[16,192,50]{1,2,0:T(8,128)S(1)} all-gather(f32[1,192,50]{1,2,0:T(8,128)} %bitcast.77), channel_id=1, replica_groups=mesh['row'=16,'col'=32] {'row'}, dimensions={0}, use_global_device_ids=true | all-gather | bytes 652800 | tf_op jit(solution)/shard_map/all_gather | solution.py:41
  79.7 0.3 copy.18
  79.9 0.3 reshape.53
  80.3 0.1 multiply_reduce_fusion.1
  80.4 0.1 multiply_reduce_fusion.2
  80.5 0.0 copy-done.3
  80.5 27.0 %while.50 = (s32[]{:T(128)}, f32[4,512]{1,0:T(4,128)S(1)}, f32[3072]{0:T(1024)S(1)}, f32[4,512]{1,0:T(4,128)S(1)}, f32[3072]{0:T(1024)S(1)}, /*index=5*/f32[4,50...) while((s32[]{:T(128)}, f32[4,512]{1,0:T(4,128)S(1)}, f32[3072]{0:T(1024)S(1)}, ...), condition=%wide.region_4.5_spmd, body=%wide.region_2.4_spmd.sunk | while | flops 953155072 | bytes 839785 | solution.py:59
  80.5 6.7 %multiply_reduce_fusion.4 = f32[512]{0:T(512)S(1)} fusion(f32[50,3072]{1,0:T(8,128)S(1)} %get-tuple-element.647, f32[3072]{0:T(1024)S(1)} %get-tuple-element.645, f32[512]{0:T(512)S(1)} %bitcast.84, f32[3072]{0:T(1024)S(1)} %get-tuple-element.643, f32[4,50,512]{2,1,0:T(8,128)S(1)} %get-tuple-element.646, s32[]{:T(128)} %get-tuple-element.632), kind=kOutput, calls=%fused_computation.clone.1 | convolution fusion | flops 953155072 | bytes 831492 | tf_op jit(solution)/shard_map/while/body/eval_jaxpr/dot_general | solution.py:21
  87.1 0.1 dynamic_update_slice.9
  87.2 6.7 %multiply_reduce_fusion.4 = f32[512]{0:T(512)S(1)} fusion(f32[50,3072]{1,0:T(8,128)S(1)} %get-tuple-element.647, f32[3072]{0:T(1024)S(1)} %get-tuple-element.645, f32[512]{0:T(512)S(1)} %bitcast.84, f32[3072]{0:T(1024)S(1)} %get-tuple-element.643, f32[4,50,512]{2,1,0:T(8,128)S(1)} %get-tuple-element.646, s32[]{:T(128)} %get-tuple-element.632), kind=kOutput, calls=%fused_computation.clone.1 | convolution fusion | flops 953155072 | bytes 831492 | tf_op jit(solution)/shard_map/while/body/eval_jaxpr/dot_general | solution.py:21
  93.9 0.1 dynamic_update_slice.9
  94.0 6.7 %multiply_reduce_fusion.4 = f32[512]{0:T(512)S(1)} fusion(f32[50,3072]{1,0:T(8,128)S(1)} %get-tuple-element.647, f32[3072]{0:T(1024)S(1)} %get-tuple-element.645, f32[512]{0:T(512)S(1)} %bitcast.84, f32[3072]{0:T(1024)S(1)} %get-tuple-element.643, f32[4,50,512]{2,1,0:T(8,128)S(1)} %get-tuple-element.646, s32[]{:T(128)} %get-tuple-element.632), kind=kOutput, calls=%fused_computation.clone.1 | convolution fusion | flops 953155072 | bytes 831492 | tf_op jit(solution)/shard_map/while/body/eval_jaxpr/dot_general | solution.py:21
  100.6 0.1 dynamic_update_slice.9
  100.7 6.7 %multiply_reduce_fusion.4 = f32[512]{0:T(512)S(1)} fusion(f32[50,3072]{1,0:T(8,128)S(1)} %get-tuple-element.647, f32[3072]{0:T(1024)S(1)} %get-tuple-element.645, f32[512]{0:T(512)S(1)} %bitcast.84, f32[3072]{0:T(1024)S(1)} %get-tuple-element.643, f32[4,50,512]{2,1,0:T(8,128)S(1)} %get-tuple-element.646, s32[]{:T(128)} %get-tuple-element.632), kind=kOutput, calls=%fused_computation.clone.1 | convolution fusion | flops 953155072 | bytes 831492 | tf_op jit(solution)/shard_map/while/body/eval_jaxpr/dot_general | solution.py:21
  107.4 0.1 dynamic_update_slice.9
  107.4 59.3 %pmax.7 = f32[2048]{0:T(1024)S(1)} all-reduce(f32[2048]{0:T(1024)S(1)} %bitcast.87), channel_id=1, replica_groups=mesh['row'=16,'col'=32] {'col'}, use_global_device_ids=true, to_apply=%region_5.6 | all-reduce | flops 2048 | bytes 16384 | tf_op jit(solution)/shard_map/pmax | solution.py:60
  166.8 0.0 copy-start.2
  166.8 29.8 %while.51 = (s32[]{:T(128)}, f32[4,512]{1,0:T(4,128)S(1)}, f32[3072]{0:T(1024)S(1)}, f32[4,512]{1,0:T(4,128)S(1)}, f32[3072]{0:T(1024)S(1)}, /*index=5*/f32[4,50...) while((s32[]{:T(128)}, f32[4,512]{1,0:T(4,128)S(1)}, ...), condition=%wide.region_8.9_spmd, body=%wide.region_6.8_spmd.sunk | while | flops 954727936 | bytes 845937 | solution.py:66
  166.8 7.4 %exponential_reduce_fusion.4 = f32[512]{0:T(512)S(1)} fusion(f32[50,3072]{1,0:T(8,128)S(1)} %get-tuple-element.676, f32[512]{0:T(512)S(1)} %bitcast.80, f32[3072]{0:T(1024)S(1)} %get-tuple-element.674, f32[512]{0:T(512)S(1)} %bitcast.81, f32[3072]{0:T(1024)S(1)} %get-tuple-element.672, f32[4,50,512]{2,1,0:T(8,128)S(1)} %get-tuple-element.675, ...), kind=kOutput, calls=%fused_computation.5.clone.1 | convolution fusion | flops 954727936 | bytes 833540 | tf_op jit(solution)/shard_map/while/body/eval_jaxpr/dot_general | solution.py:21
  174.2 0.1 dynamic_update_slice.10
  174.3 7.4 %exponential_reduce_fusion.4 = f32[512]{0:T(512)S(1)} fusion(f32[50,3072]{1,0:T(8,128)S(1)} %get-tuple-element.676, f32[512]{0:T(512)S(1)} %bitcast.80, f32[3072]{0:T(1024)S(1)} %get-tuple-element.674, f32[512]{0:T(512)S(1)} %bitcast.81, f32[3072]{0:T(1024)S(1)} %get-tuple-element.672, f32[4,50,512]{2,1,0:T(8,128)S(1)} %get-tuple-element.675, ...), kind=kOutput, calls=%fused_computation.5.clone.1 | convolution fusion | flops 954727936 | bytes 833540 | tf_op jit(solution)/shard_map/while/body/eval_jaxpr/dot_general | solution.py:21
  181.7 0.1 dynamic_update_slice.10
  181.7 7.4 %exponential_reduce_fusion.4 = f32[512]{0:T(512)S(1)} fusion(f32[50,3072]{1,0:T(8,128)S(1)} %get-tuple-element.676, f32[512]{0:T(512)S(1)} %bitcast.80, f32[3072]{0:T(1024)S(1)} %get-tuple-element.674, f32[512]{0:T(512)S(1)} %bitcast.81, f32[3072]{0:T(1024)S(1)} %get-tuple-element.672, f32[4,50,512]{2,1,0:T(8,128)S(1)} %get-tuple-element.675, ...), kind=kOutput, calls=%fused_computation.5.clone.1 | convolution fusion | flops 954727936 | bytes 833540 | tf_op jit(solution)/shard_map/while/body/eval_jaxpr/dot_general | solution.py:21
  189.1 0.1 dynamic_update_slice.10
  189.2 7.4 %exponential_reduce_fusion.4 = f32[512]{0:T(512)S(1)} fusion(f32[50,3072]{1,0:T(8,128)S(1)} %get-tuple-element.676, f32[512]{0:T(512)S(1)} %bitcast.80, f32[3072]{0:T(1024)S(1)} %get-tuple-element.674, f32[512]{0:T(512)S(1)} %bitcast.81, f32[3072]{0:T(1024)S(1)} %get-tuple-element.672, f32[4,50,512]{2,1,0:T(8,128)S(1)} %get-tuple-element.675, ...), kind=kOutput, calls=%fused_computation.5.clone.1 | convolution fusion | flops 954727936 | bytes 833540 | tf_op jit(solution)/shard_map/while/body/eval_jaxpr/dot_general | solution.py:21
  196.6 0.1 dynamic_update_slice.10
  196.6 57.2 %psum.7 = f32[2048]{0:T(1024)S(1)} all-reduce(f32[2048]{0:T(1024)S(1)} %bitcast.88), channel_id=1, replica_groups=mesh['row'=16,'col'=32] {'col'}, use_global_device_ids=true, to_apply=%region_9.10 | all-reduce | flops 2048 | bytes 16384 | tf_op jit(solution)/shard_map/psum | solution.py:67
  253.8 0.0 copy-done.2
  253.8 0.0 copy-start
  253.9 0.0 copy-start.1
  253.9 0.5 copy-done
  254.4 29.1 %while.53 = (s32[]{:T(128)}, f32[3072]{0:T(1024)S(1)}, f32[3072]{0:T(1024)S(1)}, f32[4,512]{1,0:T(4,128)S(1)}, f32[4,512]{1,0:T(4,128)S(1)}, /*index=5*/f32[3072...) while((s32[]{:T(128)}, f32[3072]{0:T(1024)S(1)}, ...), condition=%wide.region_13.14_spmd.clone, body=%wide.region_10.13_spmd.clone.sunk | while | flops 956319744 | bytes 13521015 | solution.py:84
  254.5 6.2 %fusion.26 = (f32[3072]{0:T(1024)S(1)}, f32[512,3072]{1,0:T(8,128)S(1)}) fusion(f32[50,3072]{1,0:T(8,128)S(1)} %get-tuple-element.707, f32[4,50,512]{2,1,0:T(8,128)S(1)} %get-tuple-element.706, s32[]{:T(128)} %get-tuple-element.690, f32[3072]{0:T(1024)S(1)} %get-tuple-element.705, f32[512]{0:T(512)S(1)} %bitcast.78, f32[512]{0:T(512)S(1)} %bitcast.79), kind=kOutput, calls=%fused_computation.28.clone.1 | convolution fusion | flops 953152512 | bytes 7122948 | tf_op jit(solution)/shard_map/while/body/eval_jaxpr/dot_general | solution.py:21
  260.7 1.0 exponential_reduce_fusion.5
  261.7 6.2 %fusion.26 = (f32[3072]{0:T(1024)S(1)}, f32[512,3072]{1,0:T(8,128)S(1)}) fusion(f32[50,3072]{1,0:T(8,128)S(1)} %get-tuple-element.707, f32[4,50,512]{2,1,0:T(8,128)S(1)} %get-tuple-element.706, s32[]{:T(128)} %get-tuple-element.690, f32[3072]{0:T(1024)S(1)} %get-tuple-element.705, f32[512]{0:T(512)S(1)} %bitcast.78, f32[512]{0:T(512)S(1)} %bitcast.79), kind=kOutput, calls=%fused_computation.28.clone.1 | convolution fusion | flops 953152512 | bytes 7122948 | tf_op jit(solution)/shard_map/while/body/eval_jaxpr/dot_general | solution.py:21
  268.0 1.0 exponential_reduce_fusion.5
  269.0 6.2 %fusion.26 = (f32[3072]{0:T(1024)S(1)}, f32[512,3072]{1,0:T(8,128)S(1)}) fusion(f32[50,3072]{1,0:T(8,128)S(1)} %get-tuple-element.707, f32[4,50,512]{2,1,0:T(8,128)S(1)} %get-tuple-element.706, s32[]{:T(128)} %get-tuple-element.690, f32[3072]{0:T(1024)S(1)} %get-tuple-element.705, f32[512]{0:T(512)S(1)} %bitcast.78, f32[512]{0:T(512)S(1)} %bitcast.79), kind=kOutput, calls=%fused_computation.28.clone.1 | convolution fusion | flops 953152512 | bytes 7122948 | tf_op jit(solution)/shard_map/while/body/eval_jaxpr/dot_general | solution.py:21
  275.2 1.0 exponential_reduce_fusion.5
  276.3 6.2 %fusion.26 = (f32[3072]{0:T(1024)S(1)}, f32[512,3072]{1,0:T(8,128)S(1)}) fusion(f32[50,3072]{1,0:T(8,128)S(1)} %get-tuple-element.707, f32[4,50,512]{2,1,0:T(8,128)S(1)} %get-tuple-element.706, s32[]{:T(128)} %get-tuple-element.690, f32[3072]{0:T(1024)S(1)} %get-tuple-element.705, f32[512]{0:T(512)S(1)} %bitcast.78, f32[512]{0:T(512)S(1)} %bitcast.79), kind=kOutput, calls=%fused_computation.28.clone.1 | convolution fusion | flops 953152512 | bytes 7122948 | tf_op jit(solution)/shard_map/while/body/eval_jaxpr/dot_general | solution.py:21
  282.5 1.0 exponential_reduce_fusion.5
  283.5 42.4 %all-gather = f32[49152]{0:T(1024)S(1)} all-gather(f32[3072]{0:T(1024)S(1)} %get-tuple-element.259), channel_id=2, replica_groups=mesh['row'=16,'col'=32] {'row'}, dimensions={0}, use_global_device_ids=true | all-gather | bytes 208896 | tf_op jit(solution)/shard_map/all_gather | solution.py:10
  326.0 16.6 %all-gather.1 = f32[49152]{0:T(1024)S(1)} all-gather(f32[3072]{0:T(1024)S(1)} %get-tuple-element.260), channel_id=3, replica_groups=mesh['row'=16,'col'=32] {'row'}, dimensions={0}, use_global_device_ids=true | all-gather | bytes 208896 | tf_op jit(solution)/shard_map/all_gather | solution.py:10
  342.7 1.1 while.52
  343.8 0.0 copy-done.1
  343.8 0.6 multiply_subtract_fusion
  (60 shorter events, 0.9 us)
Async XLA Ops:
  0.6 79.8 %copy-start.3 = (f32[3072]{0:T(1024)S(1)}, f32[3072]{0:T(1024)}, u32[]{:S(2)}) copy-start(f32[3072]{0:T(1024)} %param.17) | copy-start | bytes 36868
  166.8 87.0 %copy-start.2 = (f32[2048]{0:T(1024)S(1)}, f32[2048]{0:T(1024)}, u32[]{:S(2)}) copy-start(f32[2048]{0:T(1024)} %param.15) | copy-start | bytes 24580
  253.8 0.6 copy-start
  253.9 89.9 %copy-start.1 = (f32[3072]{0:T(1024)S(1)}, f32[3072]{0:T(1024)}, u32[]{:S(2)}) copy-start(f32[3072]{0:T(1024)} %param.16) | copy-start | bytes 36868
where the time goes:
time: 345 us; the launch traced here: 344 us
  blocking collectives  254 us (74%)
  matrix products  81 us (23%)
  other arithmetic  4.98 us (1%)
    dot_general x12, matrix products, cost_rows(): lax.dot_general(points_block, targets, (((0,), (0,)), ((), ())), precisio...  81 us
    pmax x1, blocking collectives, local(): row_high = lax.pmax(highs.reshape(rows), 'col')  59.3 us
    all_gather x2, blocking collectives, joined(): gathered = jax.tree.map(lambda a: lax.all_gather(a, axis), part)  59 us
    psum x1, blocking collectives, local(): row_total = lax.psum(totals.reshape(rows), 'col')  57.2 us
    all_gather x1, blocking collectives, local(): sources = lax.all_gather(src_points, 'col', axis=1, tiled=True)  40.1 us
    all_gather x1, blocking collectives, local(): targets = lax.all_gather(dst_points, 'row', axis=1, tiled=True)  38 us

commit v1 on v0

v1 whole, which is shorter than its diff:
```python
import math

import jax
import jax.numpy as jnp
from jax import lax
from jax.experimental import pallas as pl
from jax.experimental.pallas import tpu as pltpu
from jax.sharding import PartitionSpec as P

epsilon = 0.5
per_eps = math.log2(math.e) / epsilon
point_scale = math.sqrt(2.0 * per_eps)
eps_ln2 = epsilon * math.log(2.0)
log2e = math.log2(math.e)
too_large = 2.0**100
too_small = 2.0**-100
vmem_limit = 40 * 1024 * 1024

lanes = 128
half = 64
depth = 256


def lane_index(shape):
    return lax.broadcasted_iota(jnp.int32, shape, 1)


def row_index(shape):
    return lax.broadcasted_iota(jnp.int32, shape, 0)


def rounded(value):
    return value.astype(jnp.bfloat16).astype(jnp.float32)


def pieces(value):
    first = rounded(value)
    second = rounded(value - first)
    third = rounded(value - first - second)
    return first, second, third


def folded(points):
    left = jnp.concatenate([points[0:24], jnp.zeros((2, half), jnp.float32)], 0)
    return jnp.concatenate([left, points[24:50]], 1)


def unfolded(first, second):
    left = lane_index(first.shape) < half
    low = jnp.where(left, first, pltpu.roll(second, half, 1))
    high = jnp.where(left, pltpu.roll(first, half, 1), second)
    return low, high


def pack_kernel(src_ref, dst_ref, src_out, dst_out):
    odd = lax.rem(lax.axis_index("row"), 2) == 1
    src = folded(src_ref[...])
    src = jnp.concatenate([src, jnp.zeros((6, lanes), jnp.float32)], 0)
    src_out[...] = jnp.broadcast_to(src[None], src_out.shape)
    points = dst_ref[...]
    whole = jnp.where(odd, points[:, half : half + lanes], points[:, :lanes])
    rest = jnp.where(odd, points[:, :half], points[:, lanes:])
    dst_out[...] = jnp.concatenate([whole, folded(rest), jnp.zeros((4, lanes), jnp.float32)], 0)


def split(points):
    scaled = points * point_scale
    high = rounded(scaled)
    low = rounded(scaled - high)
    exact = high + low
    return high, low, jnp.sum(exact * exact, 0, keepdims=True)


def with_rows(block, first, values):
    rows = row_index(block.shape)
    for offset, value in enumerate(values):
        block = jnp.where(rows == first + offset, value, block)
    return block


def build_sources(src_ref, b_ref, norm_ref):
    pad = jnp.zeros((8, lanes), jnp.float32)
    norms = []
    for k in range(src_ref.shape[0] // 2):
        low, high = unfolded(src_ref[2 * k], src_ref[2 * k + 1])
        first, second, norm = split(jnp.concatenate([low[0:24], high], 0))
        norms.append(norm)
        extra = with_rows(first, 50, [1.0, 1.0, 1.0])
        columns = slice(lanes * k, lanes * (k + 1))
        second = jnp.concatenate([second, pad], 0).astype(jnp.bfloat16)
        b_ref[0:64, columns] = jnp.concatenate([extra, pad], 0).astype(jnp.bfloat16)
        b_ref[64:128, columns] = jnp.concatenate([first, pad], 0).astype(jnp.bfloat16)
        b_ref[128:192, columns] = second
        b_ref[192:256, columns] = second
    norm_ref[...] = jnp.concatenate(norms, 0)


def build_targets(dst_ref, potential_ref, a_ref):
    pad = jnp.zeros((8, lanes), jnp.float32)
    gap = jnp.zeros((6, lanes), jnp.float32)
    for pair in range(dst_ref.shape[0] // 2):
        even = dst_ref[2 * pair]
        odd = dst_ref[2 * pair + 1]
        low, high = unfolded(even[50:76], odd[50:76])
        middle = jnp.concatenate([low[0:24], high], 0)
        for part, points in enumerate([even[0:50], middle, odd[0:50]]):
            tile = 3 * pair + part
            first, second, norm = split(jnp.concatenate([points, gap], 0))
            bias = potential_ref[tile : tile + 1, :] * per_eps - 0.5 * norm
            extra = with_rows(first, 50, list(pieces(bias)) + [1.0, 1.0, 1.0])
            turned = jnp.concatenate([extra, pad, second, pad], 0).T
            column = lane_index(turned.shape)
            plain = jnp.where((column >= 50) & (column < 56), 0.0, turned)
            rows = slice(lanes * tile, lanes * (tile + 1))
            a_ref[rows, 0:lanes] = turned.astype(jnp.bfloat16)
            a_ref[rows, lanes : 2 * lanes] = plain.astype(jnp.bfloat16)


def dot(left, right):
    return jnp.dot(left, right, preferred_element_type=jnp.float32)


def biased_rows(rows16, bias):
    block = with_rows(rows16.astype(jnp.float32), 5, pieces(bias))
    return block.astype(jnp.bfloat16)


def as_tiles(row):
    return jnp.concatenate(
        [row[:, lanes * k : lanes * (k + 1)] for k in range(row.shape[1] // lanes)], 0
    )


def as_row(tiles):
    return jnp.concatenate([tiles[k : k + 1, :] for k in range(tiles.shape[0])], 1)


def source_kernel(src_ref, dst_ref, potential_ref, lse_ref, a_ref, b_ref, norm_ref, sum_ref):
    build_sources(src_ref, b_ref, norm_ref)
    build_targets(dst_ref, potential_ref, a_ref)
    targets = a_ref.shape[0]
    sources = b_ref.shape[1]
    width = 256
    chunk = 512
    shift = jnp.concatenate(
        [
            jnp.max(dot(a_ref[0:lanes, :], b_ref[:, width * n : width * (n + 1)]), 0, keepdims=True)
            for n in range(sources // width)
        ],
        1,
    )
    b_ref[48:64, :] = biased_rows(b_ref[48:64, :], -shift)
    for n in range(sources // width):
        columns = slice(width * n, width * (n + 1))
        block = b_ref[:, columns]

        def add(step, total):
            rows = pl.ds(pl.multiple_of(step * chunk, chunk), chunk)
            terms = jnp.exp2(dot(a_ref[rows, :], block))
            return total + jnp.sum(terms.reshape(chunk // 8, 8, width), 0)

        total = lax.fori_loop(0, targets // chunk, add, jnp.zeros((8, width), jnp.float32))
        sum_ref[0:1, columns] = jnp.sum(total, 0, keepdims=True)
    total = sum_ref[0:1, :]
    sum_ref[1:2, :] = shift + jnp.log2(total)

    @pl.when(jnp.logical_not(jnp.max(jnp.where(total <= too_large, 0.0, 1.0)) < 0.5))
    def exact():
        for n in range(sources // width):
            columns = slice(width * n, width * (n + 1))
            block = b_ref[:, columns]

            def rows_of(step):
                return pl.ds(pl.multiple_of(step * lanes, lanes), lanes)

            def highest(step, high):
                scores = dot(a_ref[rows_of(step), :], block)
                return jnp.maximum(high, jnp.max(scores, 0, keepdims=True))

            high = lax.fori_loop(
                0, targets // lanes, highest, jnp.full((1, width), -jnp.inf, jnp.float32)
            )

            def add(step, total):
                scores = dot(a_ref[rows_of(step), :], block)
                return total + jnp.sum(jnp.exp2(scores - high), 0, keepdims=True)

            total = lax.fori_loop(0, targets // lanes, add, jnp.zeros((1, width), jnp.float32))
            sum_ref[1:2, columns] = shift[:, columns] + (high + jnp.log2(total))

    lse_ref[...] = jnp.broadcast_to(as_tiles(sum_ref[1:2, :])[None], lse_ref.shape)


def target_kernel(lse_ref, log_a_ref, norm_ref, a_ref, b_ref, src_out, lse_out, acc_ref):
    targets = a_ref.shape[0]
    sources = b_ref.shape[1]
    width = 256
    chunk = 512
    parts = lse_ref[...]
    high = jnp.max(parts, 0)
    lse = high + jnp.log2(jnp.sum(jnp.exp2(parts - high[None]), 0))
    src_out[...] = epsilon * log_a_ref[...] - eps_ln2 * (lse - 0.5 * norm_ref[...])
    middle = biased_rows(b_ref[48:64, :], as_row(log2e * log_a_ref[...] - lse))

    def block_of(n):
        columns = slice(width * n, width * (n + 1))
        return jnp.concatenate(
            [b_ref[0:48, columns], middle[:, columns], b_ref[64:depth, columns]], 0
        )

    for n in range(sources // width):
        block = block_of(n)

        def add(step, carry):
            rows = pl.ds(pl.multiple_of(step * chunk, chunk), chunk)
            terms = jnp.exp2(dot(a_ref[rows, :], block))
            terms = terms[:, 0:lanes] + terms[:, lanes:]
            acc_ref[rows, :] = terms if n == 0 else acc_ref[rows, :] + terms
            return carry

        lax.fori_loop(0, targets // chunk, add, 0)
    totals = jnp.concatenate(
        [
            jnp.sum(acc_ref[lanes * t : lanes * (t + 1), :].T, 0, keepdims=True)
            for t in range(targets // lanes)
        ],
        0,
    )
    lse_out[...] = jnp.log2(totals)

    @pl.when(jnp.logical_not(jnp.max(jnp.where(totals >= too_small, 0.0, 1.0)) < 0.5))
    def exact():
        def one(tile, carry):
            left = a_ref[pl.ds(pl.multiple_of(tile * lanes, lanes), lanes), :]
            high = jnp.full((lanes, 1), -jnp.inf, jnp.float32)
            for n in range(sources // width):
                scores = dot(left, block_of(n))
                high = jnp.maximum(high, jnp.max(scores, 1, keepdims=True))
            total = jnp.zeros((lanes, 1), jnp.float32)
            for n in range(sources // width):
                scores = dot(left, block_of(n))
                total = total + jnp.sum(jnp.exp2(scores - high), 1, keepdims=True)
            result = jnp.broadcast_to(high + jnp.log2(total), (lanes, lanes)).T
            lse_out[pl.ds(tile, 1), :] = result[0:1, :]
            return carry

        lax.fori_loop(0, targets // lanes, one, 0)


def join_kernel(lse_ref, log_b_ref, potential_ref, out_ref):
    parts = lse_ref[...]
    high = jnp.max(parts, 0)
    lse = high + jnp.log2(jnp.sum(jnp.exp2(parts - high[None]), 0))
    out_ref[...] = epsilon * log_b_ref[...] + potential_ref[...] - eps_ln2 * lse


def shape(*dims, dtype=jnp.float32):
    return jax.ShapeDtypeStruct(dims, dtype)


def call(kernel, outs, scratch=(), cost=None):
    vmem = pl.BlockSpec(memory_space=pltpu.VMEM)
    many = isinstance(outs, tuple)
    return pl.pallas_call(
        kernel,
        out_shape=outs,
        out_specs=tuple(vmem for _ in outs) if many else vmem,
        scratch_shapes=scratch,
        compiler_params=pltpu.CompilerParams(vmem_limit_bytes=vmem_limit),
        cost_estimate=cost,
    )


def local(src_points, dst_points, log_a, log_b, dst_potential):
    rows = lax.axis_size("row")
    cols = lax.axis_size("col")
    sources = log_a.shape[0]
    targets = log_b.shape[0]
    log_a = log_a.reshape(sources // lanes, lanes)
    log_b = log_b.reshape(targets // lanes, lanes)
    potential = dst_potential.reshape(targets // lanes, lanes)
    pairs = sources * targets
    cost = pl.CostEstimate(
        flops=2 * depth * pairs, transcendentals=pairs, bytes_accessed=4 * depth * (sources + targets)
    )

    src, dst = call(pack_kernel, (shape(cols, 32, lanes), shape(80, lanes)))(src_points, dst_points)
    src = lax.all_to_all(src, "col", 0, 0, tiled=True)
    dst = lax.all_gather(dst, "row")

    lse, a, b, norms = call(
        source_kernel,
        (
            shape(cols, sources // lanes, lanes),
            shape(targets, depth, dtype=jnp.bfloat16),
            shape(depth, sources, dtype=jnp.bfloat16),
            shape(sources // lanes, lanes),
        ),
        [pltpu.VMEM((8, sources), jnp.float32)],
        cost,
    )(src, dst, potential)

    lse = lax.all_to_all(lse, "col", 0, 0, tiled=True)
    src_potential, lse = call(
        target_kernel,
        (shape(sources // lanes, lanes), shape(targets // lanes, lanes)),
        [pltpu.VMEM((targets, lanes), jnp.float32)],
        cost,
    )(lse, log_a, norms, a, b)

    lse = lax.all_gather(lse, "row")
    new_potential = call(join_kernel, shape(targets // lanes, lanes))(lse, log_b, potential)
    return src_potential.reshape(sources), new_potential.reshape(targets)


def solution(mesh):
    return jax.shard_map(
        local,
        mesh=mesh,
        in_specs=(P(None, ("row", "col")), P(None, ("col", "row")), P("row"), P("col"), P("col")),
        out_specs=(P("row"), P("col")),
        check_vma=False,
    )
```

time: 345 us -> 193 us (0.56)
  blocking collectives: 254 us -> 63.5 us
  Pallas kernels: 0 us -> 117 us
  matrix products: 81 us -> 0 us
  starting transfers between devices: 0 us -> 10.5 us
  other arithmetic: 4.98 us -> 0 us
    pallas_call x0 -> x4, Pallas kernels: none -> 117 us  [the longest x1 87.2 us: local(): call(source_kernel, (shape(cols, sources // lanes, lanes), shape(targets,...]
    all_gather x4 -> x2, blocking collectives: 137 us -> 42.4 us  [the longest x1 25.7 us: local(): dst = lax.all_gather(dst, 'row')]
    dot_general x12 -> x0, matrix products: 81 us -> none  [cost_rows(): lax.dot_general(points_block, targets, (((0,), (0,)), ((), ())), precisio...]
    pmax x1 -> x0, blocking collectives: 59.3 us -> none  [local(): row_high = lax.pmax(highs.reshape(rows), 'col')]
    psum x1 -> x0, blocking collectives: 57.2 us -> none  [local(): row_total = lax.psum(totals.reshape(rows), 'col')]
    all_to_all x0 -> x1, blocking collectives: none -> 21.1 us  [local(): lse = lax.all_to_all(lse, 'col', 0, 0, tiled=True)]
    all_to_all x0 -> x1, starting transfers between devices: none -> 10.5 us  [local(): src = lax.all_to_all(src, 'col', 0, 0, tiled=True)]
    reduce_sum x6 -> x0, other arithmetic: 4.05 us -> none  [the longest x4 3.92 us: advance(): summed = jnp.sum(jnp.exp(scores - highest[None, :]), 0)]
  transfers between devices with their start and end apart: 0 -> 1, of which waited for: 0 -> 0; matrix products, arithmetic and copies ran while one was open for 0% -> 0% of each run, Pallas kernels for 0% -> 0%
where the time goes in v1:
time: 193 us
  Pallas kernels  117 us (61%)
  blocking collectives  63.5 us (33%)
  starting transfers between devices  10.5 us (5%)
    pallas_call x1, Pallas kernels, local(): call(source_kernel, (shape(cols, sources // lanes, lanes), shape(targets,...  87.2 us
    pallas_call x1, Pallas kernels, local(): call(target_kernel, (shape(sources // lanes, lanes), shape(targets // lan...  27.9 us
    all_gather x1, blocking collectives, local(): dst = lax.all_gather(dst, 'row')  25.7 us
    all_to_all x1, blocking collectives, local(): lse = lax.all_to_all(lse, 'col', 0, 0, tiled=True)  21.1 us
    all_gather x1, blocking collectives, local(): lse = lax.all_gather(lse, 'row')  16.7 us
    all_to_all x1, starting transfers between devices, local(): src = lax.all_to_all(src, 'col', 0, 0, tiled=True)  10.5 us
  transfers between devices with their start and end apart: 1, of which 0 were waited for; matrix products, arithmetic and copies ran while one was open for 0% of the time, Pallas kernels for 0%

profile of v1, /device:TPU:1, one launch (start us, length us, event | category | flops | bytes accessed | tf_op | source)
XLA Modules:
  0.0 193.0 jit_solution(2753945872740557001)
XLA Ops:
  0.6 0.0 copy-start
  0.6 0.8 copy-done
  1.4 0.0 copy-start.1
  1.5 0.7 copy-done.1
  2.2 0.0 copy-start.2
  2.2 1.0 shard_map.68
  3.2 10.5 %all-to-all-start = ((f32[32,32,128]{2,1,0:T(8,128)}), f32[32,32,128]{2,1,0:T(8,128)S(1)}, u32[]{:S(2)}, u32[]{:S(2)}) async-start(f32[32,32,128]{2,1,0:T(8,128)} %get-tuple-element.10), calls=%async_computation | async-start | bytes 1048576 | tf_op jit(solution)/shard_map/all_to_all | solution.py:288
  13.7 25.7 %all-gather = f32[1280,128]{1,0:T(8,128)S(1)} all-gather(f32[80,128]{1,0:T(8,128)S(1)} %get-tuple-element.11), channel_id=2, replica_groups=mesh['row'=16,'col'=32] {'row'}, dimensions={0}, use_global_device_ids=true | all-gather | bytes 696320 | tf_op jit(solution)/shard_map/all_gather | solution.py:289
  39.5 0.0 all-to-all-done.src_ref
  39.5 0.0 copy-done.2
  39.5 0.0 copy-start.4
  39.5 87.2 %shard_map.69 = (f32[32,16,128]{2,1,0:T(8,128)S(1)}, bf16[3072,256]{1,0:T(8,128)(2,1)S(1)}, bf16[256,2048]{1,0:T(8,128)(2,1)S(1)}, f32[16,128]{1,0:T(8,128)S(1)}) custom-call(f32[32,32,128]{2,1,0:T(8,128)S(1)} %all-to-all-done.src_ref, f32[16,80,128]{2,1,0:T(8,128)S(1)} %bitcast.8, f32[24,128]{1,0:T(8,128)S(1)} %bitcast.9), custom_call_target="tpu_custom_call" | custom-call | flops 3221225472 | bytes 5242880 | tf_op jit(solution)/shard_map/pallas_call | solution.py:291
  126.6 21.1 %all_to_all.10.lse_ref = f32[32,16,128]{2,1,0:T(8,128)S(1)} all-to-all(f32[32,16,128]{2,1,0:T(8,128)S(1)} %get-tuple-element.12), channel_id=1, replica_groups=mesh['row'=16,'col'=32] {'col'}, dimensions={0} | all-to-all | bytes 524288 | tf_op jit(solution)/shard_map/all_to_all | solution.py:303
  147.8 0.0 copy-done.4
  147.8 0.0 copy-start.3
  147.8 27.9 %shard_map.70 = (f32[16,128]{1,0:T(8,128)}, f32[24,128]{1,0:T(8,128)S(1)}) custom-call(f32[32,16,128]{2,1,0:T(8,128)S(1)} %all_to_all.10.lse_ref, f32[16,128]{1,0:T(8,128)S(1)} %bitcast.12, f32[16,128]{1,0:T(8,128)S(1)} %get-tuple-element.13.norm_ref, bf16[3072,256]{1,0:T(8,128)(2,1)S(1)} %get-tuple-element.14.a_ref, ...), custom_call_target="tpu_custom_call" | custom-call | flops 3221225472 | bytes 5242880 | tf_op jit(solution)/shard_map/pallas_call | solution.py:304
  175.7 16.7 %all-gather.1 = f32[384,128]{1,0:T(8,128)S(1)} all-gather(f32[24,128]{1,0:T(8,128)S(1)} %get-tuple-element.17), channel_id=3, replica_groups=mesh['row'=16,'col'=32] {'row'}, dimensions={0}, use_global_device_ids=true | all-gather | bytes 208896 | tf_op jit(solution)/shard_map/all_gather | solution.py:311
  192.4 0.0 copy-done.3
  192.4 0.7 shard_map.71
Async XLA Ops:
  0.6 0.8 copy-start
  1.4 0.7 copy-start.1
  2.2 37.3 %copy-start.2 = (f32[3072]{0:T(1024)S(1)}, f32[3072]{0:T(1024)}, u32[]{:S(2)}) copy-start(f32[3072]{0:T(1024)} %param.9) | copy-start | bytes 36868
  3.2 36.3 %all-to-all-start = ((f32[32,32,128]{2,1,0:T(8,128)}), f32[32,32,128]{2,1,0:T(8,128)S(1)}, u32[]{:S(2)}, u32[]{:S(2)}) async-start(f32[32,32,128]{2,1,0:T(8,128)} %get-tuple-element.10), calls=%async_computation | async-start | bytes 1048576 | tf_op jit(solution)/shard_map/all_to_all | solution.py:288
  39.5 108.3 %copy-start.4 = (f32[2048]{0:T(1024)S(1)}, f32[2048]{0:T(1024)}, u32[]{:S(2)}) copy-start(f32[2048]{0:T(1024)} %param.7) | copy-start | bytes 24580
  147.8 44.6 %copy-start.3 = (f32[3072]{0:T(1024)S(1)}, f32[3072]{0:T(1024)}, u32[]{:S(2)}) copy-start(f32[3072]{0:T(1024)} %param.8) | copy-start | bytes 36868

commit v2 on v1

--- a/solution.py
+++ b/solution.py
@@ -141,7 +141,6 @@
     targets = a_ref.shape[0]
     sources = b_ref.shape[1]
     width = 256
-    chunk = 512
     shift = jnp.concatenate(
         [
             jnp.max(dot(a_ref[0:lanes, :], b_ref[:, width * n : width * (n + 1)]), 0, keepdims=True)
@@ -152,14 +151,8 @@
     b_ref[48:64, :] = biased_rows(b_ref[48:64, :], -shift)
     for n in range(sources // width):
         columns = slice(width * n, width * (n + 1))
-        block = b_ref[:, columns]
-
-        def add(step, total):
-            rows = pl.ds(pl.multiple_of(step * chunk, chunk), chunk)
-            terms = jnp.exp2(dot(a_ref[rows, :], block))
-            return total + jnp.sum(terms.reshape(chunk // 8, 8, width), 0)
-
-        total = lax.fori_loop(0, targets // chunk, add, jnp.zeros((8, width), jnp.float32))
+        terms = jnp.exp2(dot(a_ref[...], b_ref[:, columns]))
+        total = jnp.sum(terms.reshape(targets // 8, 8, width), 0)
         sum_ref[0:1, columns] = jnp.sum(total, 0, keepdims=True)
     total = sum_ref[0:1, :]
     sum_ref[1:2, :] = shift + jnp.log2(total)
@@ -195,7 +188,6 @@
     targets = a_ref.shape[0]
     sources = b_ref.shape[1]
     width = 256
-    chunk = 512
     parts = lse_ref[...]
     high = jnp.max(parts, 0)
     lse = high + jnp.log2(jnp.sum(jnp.exp2(parts - high[None]), 0))
@@ -209,16 +201,9 @@
         )
 
     for n in range(sources // width):
-        block = block_of(n)
-
-        def add(step, carry):
-            rows = pl.ds(pl.multiple_of(step * chunk, chunk), chunk)
-            terms = jnp.exp2(dot(a_ref[rows, :], block))
-            terms = terms[:, 0:lanes] + terms[:, lanes:]
-            acc_ref[rows, :] = terms if n == 0 else acc_ref[rows, :] + terms
-            return carry
-
-        lax.fori_loop(0, targets // chunk, add, 0)
+        terms = jnp.exp2(dot(a_ref[...], block_of(n)))
+        terms = terms[:, 0:lanes] + terms[:, lanes:]
+        acc_ref[...] = terms if n == 0 else acc_ref[...] + terms
     totals = jnp.concatenate(
         [
             jnp.sum(acc_ref[lanes * t : lanes * (t + 1), :].T, 0, keepdims=True)

time: 193 us -> 175 us (0.907)
  Pallas kernels: 117 us -> 98.6 us
    pallas_call x1, Pallas kernels: 87.2 us -> 77.4 us  [local(): call(source_kernel, (shape(cols, sources // lanes, lanes), shape(targets,...]
    pallas_call x1, Pallas kernels: 27.9 us -> 19.6 us  [local(): call(target_kernel, (shape(sources // lanes, lanes), shape(targets // lan...]
where the time goes in v2:
time: 175 us
  Pallas kernels  98.6 us (56%)
  blocking collectives  63.6 us (36%)
  starting transfers between devices  10.5 us (6%)
    pallas_call x1, Pallas kernels, local(): call(source_kernel, (shape(cols, sources // lanes, lanes), shape(targets,...  77.4 us
    all_gather x1, blocking collectives, local(): dst = lax.all_gather(dst, 'row')  25.7 us
    all_to_all x1, blocking collectives, local(): lse = lax.all_to_all(lse, 'col', 0, 0, tiled=True)  21.1 us
    pallas_call x1, Pallas kernels, local(): call(target_kernel, (shape(sources // lanes, lanes), shape(targets // lan...  19.6 us
    all_gather x1, blocking collectives, local(): lse = lax.all_gather(lse, 'row')  16.8 us
    all_to_all x1, starting transfers between devices, local(): src = lax.all_to_all(src, 'col', 0, 0, tiled=True)  10.5 us
  transfers between devices with their start and end apart: 1, of which 0 were waited for; matrix products, arithmetic and copies ran while one was open for 0% of the time, Pallas kernels for 0%

profile of v2, /device:TPU:1, one launch (start us, length us, event | category | flops | bytes accessed | tf_op | source)
XLA Modules:
  0.0 174.9 jit_solution(2500770860251186270)
XLA Ops:
  0.6 0.0 copy-start
  0.6 0.8 copy-done
  1.4 0.0 copy-start.1
  1.5 0.7 copy-done.1
  2.2 0.0 copy-start.2
  2.2 1.0 shard_map.68
  3.2 10.5 %all-to-all-start = ((f32[32,32,128]{2,1,0:T(8,128)}), f32[32,32,128]{2,1,0:T(8,128)S(1)}, u32[]{:S(2)}, u32[]{:S(2)}) async-start(f32[32,32,128]{2,1,0:T(8,128)} %get-tuple-element.10), calls=%async_computation | async-start | bytes 1048576 | tf_op jit(solution)/shard_map/all_to_all | solution.py:273
  13.7 25.7 %all-gather = f32[1280,128]{1,0:T(8,128)S(1)} all-gather(f32[80,128]{1,0:T(8,128)S(1)} %get-tuple-element.11), channel_id=2, replica_groups=mesh['row'=16,'col'=32] {'row'}, dimensions={0}, use_global_device_ids=true | all-gather | bytes 696320 | tf_op jit(solution)/shard_map/all_gather | solution.py:274
  39.5 0.0 all-to-all-done.src_ref
  39.5 0.0 copy-done.2
  39.5 0.0 copy-start.4
  39.5 77.4 %shard_map.69 = (f32[32,16,128]{2,1,0:T(8,128)S(1)}, bf16[3072,256]{1,0:T(8,128)(2,1)S(1)}, bf16[256,2048]{1,0:T(8,128)(2,1)S(1)}, f32[16,128]{1,0:T(8,128)S(1)}) custom-call(f32[32,32,128]{2,1,0:T(8,128)S(1)} %all-to-all-done.src_ref, f32[16,80,128]{2,1,0:T(8,128)S(1)} %bitcast.8, f32[24,128]{1,0:T(8,128)S(1)} %bitcast.9), custom_call_target="tpu_custom_call" | custom-call | flops 3221225472 | bytes 5242880 | tf_op jit(solution)/shard_map/pallas_call | solution.py:276
  116.8 21.1 %all_to_all.10.lse_ref = f32[32,16,128]{2,1,0:T(8,128)S(1)} all-to-all(f32[32,16,128]{2,1,0:T(8,128)S(1)} %get-tuple-element.12), channel_id=1, replica_groups=mesh['row'=16,'col'=32] {'col'}, dimensions={0} | all-to-all | bytes 524288 | tf_op jit(solution)/shard_map/all_to_all | solution.py:288
  138.0 0.0 copy-done.4
  138.0 0.0 copy-start.3
  138.0 19.6 %shard_map.70 = (f32[16,128]{1,0:T(8,128)}, f32[24,128]{1,0:T(8,128)S(1)}) custom-call(f32[32,16,128]{2,1,0:T(8,128)S(1)} %all_to_all.10.lse_ref, f32[16,128]{1,0:T(8,128)S(1)} %bitcast.12, f32[16,128]{1,0:T(8,128)S(1)} %get-tuple-element.13.norm_ref, bf16[3072,256]{1,0:T(8,128)(2,1)S(1)} %get-tuple-element.14.a_ref, ...), custom_call_target="tpu_custom_call" | custom-call | flops 3221225472 | bytes 5242880 | tf_op jit(solution)/shard_map/pallas_call | solution.py:289
  157.5 16.8 %all-gather.1 = f32[384,128]{1,0:T(8,128)S(1)} all-gather(f32[24,128]{1,0:T(8,128)S(1)} %get-tuple-element.17), channel_id=3, replica_groups=mesh['row'=16,'col'=32] {'row'}, dimensions={0}, use_global_device_ids=true | all-gather | bytes 208896 | tf_op jit(solution)/shard_map/all_gather | solution.py:296
  174.3 0.0 copy-done.3
  174.3 0.7 shard_map.71
Async XLA Ops:
  0.6 0.8 copy-start
  1.4 0.7 copy-start.1
  2.2 37.3 %copy-start.2 = (f32[3072]{0:T(1024)S(1)}, f32[3072]{0:T(1024)}, u32[]{:S(2)}) copy-start(f32[3072]{0:T(1024)} %param.9) | copy-start | bytes 36868
  3.2 36.3 %all-to-all-start = ((f32[32,32,128]{2,1,0:T(8,128)}), f32[32,32,128]{2,1,0:T(8,128)S(1)}, u32[]{:S(2)}, u32[]{:S(2)}) async-start(f32[32,32,128]{2,1,0:T(8,128)} %get-tuple-element.10), calls=%async_computation | async-start | bytes 1048576 | tf_op jit(solution)/shard_map/all_to_all | solution.py:273
  39.5 98.5 %copy-start.4 = (f32[2048]{0:T(1024)S(1)}, f32[2048]{0:T(1024)}, u32[]{:S(2)}) copy-start(f32[2048]{0:T(1024)} %param.7) | copy-start | bytes 24580
  138.0 36.3 %copy-start.3 = (f32[3072]{0:T(1024)S(1)}, f32[3072]{0:T(1024)}, u32[]{:S(2)}) copy-start(f32[3072]{0:T(1024)} %param.8) | copy-start | bytes 36868

commit v3 on v2

--- a/solution.py
+++ b/solution.py
@@ -14,7 +14,8 @@
 log2e = math.log2(math.e)
 too_large = 2.0**100
 too_small = 2.0**-100
-vmem_limit = 40 * 1024 * 1024
+vmem_limit = 32 * 1024 * 1024
+vmem_whole = 60 * 1024 * 1024
 
 lanes = 128
 half = 64
@@ -52,15 +53,45 @@
     return low, high
 
 
-def pack_kernel(src_ref, dst_ref, src_out, dst_out):
-    odd = lax.rem(lax.axis_index("row"), 2) == 1
-    src = folded(src_ref[...])
-    src = jnp.concatenate([src, jnp.zeros((6, lanes), jnp.float32)], 0)
+def pack_kernel(src_hbm, dst_hbm, src_out, dst_out, src_ref, dst_ref, src_sem, dst_sem):
+    src_copy = pltpu.make_async_copy(src_hbm, src_ref, src_sem)
+    dst_copy = pltpu.make_async_copy(dst_hbm, dst_ref, dst_sem)
+    src_copy.start()
+    dst_copy.start()
+    src_copy.wait()
+    src = jnp.concatenate([folded(src_ref[...]), jnp.zeros((6, lanes), jnp.float32)], 0)
     src_out[...] = jnp.broadcast_to(src[None], src_out.shape)
-    points = dst_ref[...]
-    whole = jnp.where(odd, points[:, half : half + lanes], points[:, :lanes])
-    rest = jnp.where(odd, points[:, :half], points[:, lanes:])
-    dst_out[...] = jnp.concatenate([whole, folded(rest), jnp.zeros((4, lanes), jnp.float32)], 0)
+    dst_copy.wait()
+    dst_out[0:50, :] = dst_ref[:, :lanes]
+    dst_out[50:76, :] = folded(dst_ref[:, lanes:])
+    dst_out[76:80, :] = jnp.zeros((4, lanes), jnp.float32)
+
+
+def swapped(rows):
+    return pltpu.roll(rows, half, 1)
+
+
+def inner_order(tiles):
+    left = lane_index((1, lanes)) < half
+    rows = []
+    for t in range(0, tiles.shape[0], 3):
+        second, third = tiles[t + 1 : t + 2], tiles[t + 2 : t + 3]
+        rows.append(tiles[t : t + 1])
+        rows.append(jnp.where(left, second, third))
+        rows.append(swapped(jnp.where(left, third, second)))
+    return jnp.concatenate(rows, 0)
+
+
+def outer_order(tiles):
+    left = lane_index((1, lanes)) < half
+    turned = swapped(tiles)
+    rows = []
+    for t in range(0, tiles.shape[0], 3):
+        second, third = tiles[t + 1 : t + 2], turned[t + 2 : t + 3]
+        rows.append(tiles[t : t + 1])
+        rows.append(jnp.where(left, second, third))
+        rows.append(jnp.where(left, third, second))
+    return jnp.concatenate(rows, 0)
 
 
 def split(points):
@@ -98,6 +129,7 @@
 def build_targets(dst_ref, potential_ref, a_ref):
     pad = jnp.zeros((8, lanes), jnp.float32)
     gap = jnp.zeros((6, lanes), jnp.float32)
+    potential = inner_order(potential_ref[...])
     for pair in range(dst_ref.shape[0] // 2):
         even = dst_ref[2 * pair]
         odd = dst_ref[2 * pair + 1]
@@ -106,7 +138,7 @@
         for part, points in enumerate([even[0:50], middle, odd[0:50]]):
             tile = 3 * pair + part
             first, second, norm = split(jnp.concatenate([points, gap], 0))
-            bias = potential_ref[tile : tile + 1, :] * per_eps - 0.5 * norm
+            bias = potential[tile : tile + 1, :] * per_eps - 0.5 * norm
             extra = with_rows(first, 50, list(pieces(bias)) + [1.0, 1.0, 1.0])
             turned = jnp.concatenate([extra, pad, second, pad], 0).T
             column = lane_index(turned.shape)
@@ -211,7 +243,7 @@
         ],
         0,
     )
-    lse_out[...] = jnp.log2(totals)
+    lse_out[...] = jnp.broadcast_to(jnp.log2(totals)[None], lse_out.shape)
 
     @pl.when(jnp.logical_not(jnp.max(jnp.where(totals >= too_small, 0.0, 1.0)) < 0.5))
     def exact():
@@ -226,7 +258,9 @@
                 scores = dot(left, block_of(n))
                 total = total + jnp.sum(jnp.exp2(scores - high), 1, keepdims=True)
             result = jnp.broadcast_to(high + jnp.log2(total), (lanes, lanes)).T
-            lse_out[pl.ds(tile, 1), :] = result[0:1, :]
+            lse_out[:, pl.ds(tile, 1), :] = jnp.broadcast_to(
+                result[None, 0:1, :], (lse_out.shape[0], 1, lanes)
+            )
             return carry
 
         lax.fori_loop(0, targets // lanes, one, 0)
@@ -236,14 +270,16 @@
     parts = lse_ref[...]
     high = jnp.max(parts, 0)
     lse = high + jnp.log2(jnp.sum(jnp.exp2(parts - high[None]), 0))
-    out_ref[...] = epsilon * log_b_ref[...] + potential_ref[...] - eps_ln2 * lse
+    out_ref[...] = (
+        epsilon * log_b_ref[...] + potential_ref[...] - eps_ln2 * outer_order(lse)
+    )
 
 
 def shape(*dims, dtype=jnp.float32):
     return jax.ShapeDtypeStruct(dims, dtype)
 
 
-def call(kernel, outs, scratch=(), cost=None):
+def call(kernel, outs, scratch=(), cost=None, ins=None, limit=vmem_limit):
     vmem = pl.BlockSpec(memory_space=pltpu.VMEM)
     many = isinstance(outs, tuple)
     return pl.pallas_call(
@@ -251,8 +287,9 @@
         out_shape=outs,
         out_specs=tuple(vmem for _ in outs) if many else vmem,
         scratch_shapes=scratch,
-        compiler_params=pltpu.CompilerParams(vmem_limit_bytes=vmem_limit),
+        compiler_params=pltpu.CompilerParams(vmem_limit_bytes=limit),
         cost_estimate=cost,
+        **({} if ins is None else {"in_specs": ins}),
     )
 
 
@@ -269,7 +306,18 @@
         flops=2 * depth * pairs, transcendentals=pairs, bytes_accessed=4 * depth * (sources + targets)
     )
 
-    src, dst = call(pack_kernel, (shape(cols, 32, lanes), shape(80, lanes)))(src_points, dst_points)
+    src, dst = call(
+        pack_kernel,
+        (shape(cols, 32, lanes), shape(80, lanes)),
+        [
+            pltpu.VMEM(src_points.shape, jnp.float32),
+            pltpu.VMEM(dst_points.shape, jnp.float32),
+            pltpu.SemaphoreType.DMA,
+            pltpu.SemaphoreType.DMA,
+        ],
+        ins=[pl.BlockSpec(memory_space=pl.ANY)] * 2,
+        limit=vmem_whole,
+    )(src_points, dst_points)
     src = lax.all_to_all(src, "col", 0, 0, tiled=True)
     dst = lax.all_gather(dst, "row")
 
@@ -288,12 +336,12 @@
     lse = lax.all_to_all(lse, "col", 0, 0, tiled=True)
     src_potential, lse = call(
         target_kernel,
-        (shape(sources // lanes, lanes), shape(targets // lanes, lanes)),
+        (shape(sources // lanes, lanes), shape(rows, targets // lanes, lanes)),
         [pltpu.VMEM((targets, lanes), jnp.float32)],
         cost,
     )(lse, log_a, norms, a, b)
 
-    lse = lax.all_gather(lse, "row")
+    lse = lax.all_to_all(lse, "row", 0, 0, tiled=True)
     new_potential = call(join_kernel, shape(targets // lanes, lanes))(lse, log_b, potential)
     return src_potential.reshape(sources), new_potential.reshape(targets)
 

time: 175 us -> 173 us (0.989)
    all_gather x1 -> x0, blocking collectives: 16.8 us -> none  [local(): lse = lax.all_gather(lse, 'row')]
    all_to_all x0 -> x1, blocking collectives: none -> 15 us  [local(): lse = lax.all_to_all(lse, 'row', 0, 0, tiled=True)]
where the time goes in v3:
time: 173 us
  Pallas kernels  99.3 us (57%)
  blocking collectives  62.1 us (36%)
  starting transfers between devices  10.5 us (6%)
    pallas_call x1, Pallas kernels, local(): call(source_kernel, (shape(cols, sources // lanes, lanes), shape(targets,...  77.3 us
    all_gather x1, blocking collectives, local(): dst = lax.all_gather(dst, 'row')  26 us
    all_to_all x1, blocking collectives, local(): lse = lax.all_to_all(lse, 'col', 0, 0, tiled=True)  21.1 us
    pallas_call x1, Pallas kernels, local(): call(target_kernel, (shape(sources // lanes, lanes), shape(rows, targets...  19.6 us
    all_to_all x1, blocking collectives, local(): lse = lax.all_to_all(lse, 'row', 0, 0, tiled=True)  15 us
    all_to_all x1, starting transfers between devices, local(): src = lax.all_to_all(src, 'col', 0, 0, tiled=True)  10.5 us
  transfers between devices with their start and end apart: 1, of which 0 were waited for; matrix products, arithmetic and copies ran while one was open for 0% of the time, Pallas kernels for 0%

profile of v3, /device:TPU:1, one launch (start us, length us, event | category | flops | bytes accessed | tf_op | source)
XLA Modules:
  0.0 172.6 jit_solution(6105162826864115957)
XLA Ops:
  0.6 0.0 copy-start
  0.6 1.7 shard_map.68
  2.3 10.5 %all-to-all-start = ((f32[32,32,128]{2,1,0:T(8,128)}), f32[32,32,128]{2,1,0:T(8,128)S(1)}, u32[]{:S(2)}, u32[]{:S(2)}) async-start(f32[32,32,128]{2,1,0:T(8,128)} %get-tuple-element.10), calls=%async_computation | async-start | bytes 1048576 | tf_op jit(solution)/shard_map/all_to_all | solution.py:321
  12.9 26.0 %all-gather = f32[1280,128]{1,0:T(8,128)S(1)} all-gather(f32[80,128]{1,0:T(8,128)} %get-tuple-element.11), channel_id=2, replica_groups=mesh['row'=16,'col'=32] {'row'}, dimensions={0}, use_global_device_ids=true | all-gather | bytes 696320 | tf_op jit(solution)/shard_map/all_gather | solution.py:322
  38.9 0.0 all-to-all-done.src_ref
  38.9 0.0 copy-done
  38.9 0.0 copy-start.2
  38.9 77.3 %shard_map.69 = (f32[32,16,128]{2,1,0:T(8,128)S(1)}, bf16[3072,256]{1,0:T(8,128)(2,1)S(1)}, bf16[256,2048]{1,0:T(8,128)(2,1)S(1)}, f32[16,128]{1,0:T(8,128)S(1)}) custom-call(f32[32,32,128]{2,1,0:T(8,128)S(1)} %all-to-all-done.src_ref, f32[16,80,128]{2,1,0:T(8,128)S(1)} %bitcast.6, f32[24,128]{1,0:T(8,128)S(1)} %bitcast.7), custom_call_target="tpu_custom_call" | custom-call | flops 3221225472 | bytes 5242880 | tf_op jit(solution)/shard_map/pallas_call | solution.py:324
  116.2 21.1 %all_to_all.15.lse_ref = f32[32,16,128]{2,1,0:T(8,128)S(1)} all-to-all(f32[32,16,128]{2,1,0:T(8,128)S(1)} %get-tuple-element.12), channel_id=1, replica_groups=mesh['row'=16,'col'=32] {'col'}, dimensions={0} | all-to-all | bytes 524288 | tf_op jit(solution)/shard_map/all_to_all | solution.py:336
  137.3 0.0 copy-done.2
  137.3 0.0 copy-start.1
  137.3 19.6 %shard_map.70 = (f32[16,128]{1,0:T(8,128)}, f32[16,24,128]{2,1,0:T(8,128)S(1)}) custom-call(f32[32,16,128]{2,1,0:T(8,128)S(1)} %all_to_all.15.lse_ref, f32[16,128]{1,0:T(8,128)S(1)} %bitcast.10, f32[16,128]{1,0:T(8,128)S(1)} %get-tuple-element.13.norm_ref, bf16[3072,256]{1,0:T(8,128)(2,1)S(1)} %get-tuple-element.14.a_ref, ...), custom_call_target="tpu_custom_call" | custom-call | flops 3221225472 | bytes 5242880 | tf_op jit(solution)/shard_map/pallas_call | solution.py:337
  156.9 15.0 %all_to_all.16.lse_ref = f32[16,24,128]{2,1,0:T(8,128)S(1)} all-to-all(f32[16,24,128]{2,1,0:T(8,128)S(1)} %get-tuple-element.17), channel_id=1, replica_groups=mesh['row'=16,'col'=32] {'row'}, dimensions={0} | all-to-all | bytes 393216 | tf_op jit(solution)/shard_map/all_to_all | solution.py:344
  171.9 0.0 copy-done.1
  171.9 0.7 shard_map.71
Async XLA Ops:
  0.6 38.2 %copy-start = (f32[3072]{0:T(1024)S(1)}, f32[3072]{0:T(1024)}, u32[]{:S(2)}) copy-start(f32[3072]{0:T(1024)} %param.9) | copy-start | bytes 36868
  2.3 36.5 %all-to-all-start = ((f32[32,32,128]{2,1,0:T(8,128)}), f32[32,32,128]{2,1,0:T(8,128)S(1)}, u32[]{:S(2)}, u32[]{:S(2)}) async-start(f32[32,32,128]{2,1,0:T(8,128)} %get-tuple-element.10), calls=%async_computation | async-start | bytes 1048576 | tf_op jit(solution)/shard_map/all_to_all | solution.py:321
  38.9 98.5 %copy-start.2 = (f32[2048]{0:T(1024)S(1)}, f32[2048]{0:T(1024)}, u32[]{:S(2)}) copy-start(f32[2048]{0:T(1024)} %param.7) | copy-start | bytes 24580
  137.3 34.5 %copy-start.1 = (f32[3072]{0:T(1024)S(1)}, f32[3072]{0:T(1024)}, u32[]{:S(2)}) copy-start(f32[3072]{0:T(1024)} %param.8) | copy-start | bytes 36868

commit v4 on v3

v4 whole, which is shorter than its diff:
```python
import math

import jax
import jax.numpy as jnp
from jax import lax
from jax.experimental import pallas as pl
from jax.experimental.pallas import tpu as pltpu
from jax.sharding import PartitionSpec as P

epsilon = 0.5
per_eps = math.log2(math.e) / epsilon
point_scale = math.sqrt(2.0 * per_eps)
eps_ln2 = epsilon * math.log(2.0)
log2e = math.log2(math.e)
too_large = 2.0**40
too_small = 2.0**-50
vmem_limit = 8 * 1024 * 1024
vmem_whole = 60 * 1024 * 1024

lanes = 128
half = 64
depth = 256
width = 256


def lane_index(shape):
    return lax.broadcasted_iota(jnp.int32, shape, 1)


def row_index(shape):
    return lax.broadcasted_iota(jnp.int32, shape, 0)


def rounded(value):
    return value.astype(jnp.bfloat16).astype(jnp.float32)


def pieces(value):
    first = rounded(value)
    second = rounded(value - first)
    third = rounded(value - first - second)
    return first, second, third


def folded(points, spare):
    left = jnp.concatenate([points[0:24], spare, jnp.zeros((1, half), jnp.float32)], 0)
    return jnp.concatenate([left, points[24:50]], 1)


def unfolded(first, second):
    left = lane_index(first.shape) < half
    low = jnp.where(left, first, swapped(second))
    high = jnp.where(left, swapped(first), second)
    return low, high


def pack_kernel(
    src_hbm,
    dst_hbm,
    log_a_hbm,
    potential_hbm,
    src_out,
    dst_out,
    src_ref,
    dst_ref,
    log_a_ref,
    potential_ref,
    sems,
):
    copies = [
        pltpu.make_async_copy(source, target, sems.at[k])
        for k, (source, target) in enumerate(
            [
                (src_hbm, src_ref),
                (dst_hbm, dst_ref),
                (log_a_hbm, log_a_ref),
                (potential_hbm, potential_ref),
            ]
        )
    ]
    for copy in copies:
        copy.start()
    for copy in copies:
        copy.wait()
    col = lax.axis_index("col")
    line = log_a_ref[pl.ds(lax.div(col, 2), 1), :]
    line = jnp.where(lax.rem(col, 2) == 1, swapped(line), line)
    src = folded(src_ref[...], line[:, :half])
    src = jnp.concatenate([src, jnp.zeros((6, lanes), jnp.float32)], 0)
    src_out[...] = jnp.broadcast_to(src[None], src_out.shape)
    row = lax.axis_index("row")
    odd = lax.rem(row, 2) == 1
    base = 3 * lax.div(row, 2)
    first, second, third = [potential_ref[pl.ds(base + k, 1), :] for k in range(3)]
    left = lane_index((1, lanes)) < half
    whole = jnp.where(odd, swapped(jnp.where(left, third, second)), first)
    rest = jnp.where(odd, swapped(third), second)
    dst_out[0:50, :] = dst_ref[:, :lanes]
    dst_out[50:76, :] = folded(dst_ref[:, lanes:], rest[:, :half])
    dst_out[76:80, :] = jnp.concatenate([whole, jnp.zeros((3, lanes), jnp.float32)], 0)


def swapped(rows):
    return pltpu.roll(rows, half, 1)


def outer_order(tiles):
    left = lane_index((1, lanes)) < half
    turned = swapped(tiles)
    rows = []
    for t in range(0, tiles.shape[0], 3):
        second, third = tiles[t + 1 : t + 2], turned[t + 2 : t + 3]
        rows.append(tiles[t : t + 1])
        rows.append(jnp.where(left, second, third))
        rows.append(jnp.where(left, third, second))
    return jnp.concatenate(rows, 0)


def split(points):
    scaled = points * point_scale
    high = rounded(scaled)
    low = rounded(scaled - high)
    exact = high + low
    return high, low, jnp.sum(exact * exact, 0, keepdims=True)


def with_rows(block, first, values):
    rows = row_index(block.shape)
    for offset, value in enumerate(values):
        block = jnp.where(rows == first + offset, value, block)
    return block


def build_sources(src_ref, b_ref, norm_ref, log_a_ref):
    pad = jnp.zeros((8, lanes), jnp.float32)
    norms, weights = [], []
    for k in range(src_ref.shape[0] // 2):
        low, high = unfolded(src_ref[2 * k], src_ref[2 * k + 1])
        first, second, norm = split(jnp.concatenate([low[0:24], high], 0))
        norms.append(norm)
        weights.append(low[24:25])
        extra = with_rows(first, 50, [1.0, 1.0, 1.0])
        columns = slice(lanes * k, lanes * (k + 1))
        second = jnp.concatenate([second, pad], 0).astype(jnp.bfloat16)
        b_ref[0:64, columns] = jnp.concatenate([extra, pad], 0).astype(jnp.bfloat16)
        b_ref[64:128, columns] = jnp.concatenate([first, pad], 0).astype(jnp.bfloat16)
        b_ref[128:192, columns] = second
        b_ref[192:256, columns] = second
    norm_ref[...] = jnp.concatenate(norms, 0)
    log_a_ref[...] = jnp.concatenate(weights, 0)


def build_targets(dst_ref, a_ref):
    pad = jnp.zeros((8, lanes), jnp.float32)
    gap = jnp.zeros((6, lanes), jnp.float32)
    for pair in range(dst_ref.shape[0] // 2):
        even = dst_ref[2 * pair]
        odd = dst_ref[2 * pair + 1]
        low, high = unfolded(even[50:76], odd[50:76])
        middle = jnp.concatenate([low[0:24], high], 0)
        groups = [(even[0:50], even[76:77]), (middle, low[24:25]), (odd[0:50], odd[76:77])]
        for part, (points, potential) in enumerate(groups):
            tile = 3 * pair + part
            first, second, norm = split(jnp.concatenate([points, gap], 0))
            bias = potential * per_eps - 0.5 * norm
            extra = with_rows(first, 50, pieces(bias))
            turned = jnp.concatenate([extra, pad, second, pad], 0).T
            column = lane_index(turned.shape)
            plain = jnp.where((column >= 50) & (column < 53), 0.0, turned)
            rows = slice(lanes * tile, lanes * (tile + 1))
            a_ref[rows, 0:lanes] = turned.astype(jnp.bfloat16)
            a_ref[rows, lanes : 2 * lanes] = plain.astype(jnp.bfloat16)


def dot(left, right):
    return jnp.dot(left, right, preferred_element_type=jnp.float32)


def as_tiles(row):
    return jnp.concatenate(
        [row[:, lanes * k : lanes * (k + 1)] for k in range(row.shape[1] // lanes)], 0
    )


def as_row(tiles):
    return jnp.concatenate([tiles[k : k + 1, :] for k in range(tiles.shape[0])], 1)


def unit_block(n):
    return slice(width * n, width * (n + 1))


def source_kernel(
    src_ref, dst_ref, lse_ref, share_ref, a_ref, b_ref, norm_ref, row_ref, log_a_ref
):
    build_sources(src_ref, b_ref, norm_ref, log_a_ref)
    build_targets(dst_ref, a_ref)
    targets = a_ref.shape[0]
    blocks = b_ref.shape[1] // width
    worst = jnp.zeros((1, width), jnp.float32)
    for n in range(blocks):
        scores = dot(a_ref[...], b_ref[:, unit_block(n)])
        shift = jnp.max(scores[0:lanes], 0, keepdims=True)
        terms = jnp.exp2(scores - shift)
        share_ref[:, unit_block(n)] = terms
        total = jnp.sum(jnp.sum(terms.reshape(targets // 8, 8, width), 0), 0, keepdims=True)
        worst = jnp.maximum(worst, jnp.where(total <= too_large, 0.0, 1.0))
        row_ref[0:1, unit_block(n)] = shift
        row_ref[1:2, unit_block(n)] = shift + jnp.log2(total)

    @pl.when(jnp.max(worst) > 0.5)
    def exact():
        def rows_of(step):
            return pl.ds(pl.multiple_of(step * lanes, lanes), lanes)

        for n in range(blocks):
            block = b_ref[:, unit_block(n)]

            def highest(step, high):
                scores = dot(a_ref[rows_of(step), :], block)
                return jnp.maximum(high, jnp.max(scores, 0, keepdims=True))

            high = lax.fori_loop(
                0, targets // lanes, highest, jnp.full((1, width), -jnp.inf, jnp.float32)
            )

            def add(step, total):
                terms = jnp.exp2(dot(a_ref[rows_of(step), :], block) - high)
                share_ref[rows_of(step), unit_block(n)] = terms
                return total + jnp.sum(terms, 0, keepdims=True)

            total = lax.fori_loop(0, targets // lanes, add, jnp.zeros((1, width), jnp.float32))
            row_ref[0:1, unit_block(n)] = high
            row_ref[1:2, unit_block(n)] = high + jnp.log2(total)

    lse_ref[...] = jnp.broadcast_to(as_tiles(row_ref[1:2, :])[None], lse_ref.shape)


def target_kernel(
    lse_ref, log_a_ref, norm_ref, row_ref, share_ref, a_ref, b_ref, src_out, lse_out
):
    targets, sources = share_ref.shape
    parts = lse_ref[...]
    high = jnp.max(parts, 0)
    lse = high + jnp.log2(jnp.sum(jnp.exp2(parts - high[None]), 0))
    src_out[...] = epsilon * log_a_ref[...] - eps_ln2 * (lse - 0.5 * norm_ref[...])
    bias = log2e * log_a_ref[...] - lse
    factor = jnp.exp2(bias + as_tiles(row_ref[0:1, :]))
    totals = []
    for t in range(targets // lanes):
        rows = slice(lanes * t, lanes * (t + 1))
        block = jnp.zeros((lanes, lanes), jnp.float32)
        for k in range(sources // lanes):
            block = block + share_ref[rows, lanes * k : lanes * (k + 1)] * factor[k : k + 1, :]
        totals.append(jnp.sum(block.T, 0, keepdims=True))
    totals = jnp.concatenate(totals, 0)
    lse_out[...] = jnp.broadcast_to(jnp.log2(totals)[None], lse_out.shape)

    @pl.when(jnp.max(jnp.where(totals >= too_small, 0.0, 1.0)) > 0.5)
    def exact():
        bias_row = as_row(bias)

        def one(tile, carry):
            left = a_ref[pl.ds(pl.multiple_of(tile * lanes, lanes), lanes), :]
            high = jnp.full((lanes, 1), -jnp.inf, jnp.float32)
            for n in range(sources // width):
                scores = dot(left, b_ref[:, unit_block(n)]) + bias_row[:, unit_block(n)]
                high = jnp.maximum(high, jnp.max(scores, 1, keepdims=True))
            total = jnp.zeros((lanes, 1), jnp.float32)
            for n in range(sources // width):
                scores = dot(left, b_ref[:, unit_block(n)]) + bias_row[:, unit_block(n)]
                total = total + jnp.sum(jnp.exp2(scores - high), 1, keepdims=True)
            result = jnp.broadcast_to(high + jnp.log2(total), (lanes, lanes)).T
            lse_out[:, pl.ds(tile, 1), :] = jnp.broadcast_to(
                result[None, 0:1, :], (lse_out.shape[0], 1, lanes)
            )
            return carry

        lax.fori_loop(0, targets // lanes, one, 0)


def join_kernel(lse_ref, log_b_ref, potential_ref, out_ref):
    parts = lse_ref[...]
    high = jnp.max(parts, 0)
    lse = high + jnp.log2(jnp.sum(jnp.exp2(parts - high[None]), 0))
    out_ref[...] = (
        epsilon * log_b_ref[...] + potential_ref[...] - eps_ln2 * outer_order(lse)
    )


def shape(*dims, dtype=jnp.float32):
    return jax.ShapeDtypeStruct(dims, dtype)


def call(kernel, outs, scratch=(), cost=None, limit=vmem_limit, **kwargs):
    vmem = pl.BlockSpec(memory_space=pltpu.VMEM)
    many = isinstance(outs, tuple)
    return pl.pallas_call(
        kernel,
        out_shape=outs,
        out_specs=tuple(vmem for _ in outs) if many else vmem,
        scratch_shapes=scratch,
        compiler_params=pltpu.CompilerParams(vmem_limit_bytes=limit),
        cost_estimate=cost,
        **kwargs,
    )


def local(src_points, dst_points, log_a, log_b, dst_potential):
    rows = lax.axis_size("row")
    cols = lax.axis_size("col")
    sources = log_a.shape[0]
    targets = log_b.shape[0]
    log_a = log_a.reshape(sources // lanes, lanes)
    log_b = log_b.reshape(targets // lanes, lanes)
    potential = dst_potential.reshape(targets // lanes, lanes)
    pairs = sources * targets
    cost = pl.CostEstimate(
        flops=2 * depth * pairs, transcendentals=pairs, bytes_accessed=4 * depth * (sources + targets)
    )

    packed = (src_points, dst_points, log_a, potential)
    src, dst = call(
        pack_kernel,
        (shape(cols, 32, lanes), shape(80, lanes)),
        [pltpu.VMEM(array.shape, jnp.float32) for array in packed]
        + [pltpu.SemaphoreType.DMA((len(packed),))],
        limit=vmem_whole,
        in_specs=[pl.BlockSpec(memory_space=pltpu.HBM)] * len(packed),
    )(*packed)
    src = lax.all_to_all(src, "col", 0, 0, tiled=True)
    dst = lax.all_gather(dst, "row")

    lse, share, a, b, norms, row, log_a = call(
        source_kernel,
        (
            shape(cols, sources // lanes, lanes),
            shape(targets, sources),
            shape(targets, depth, dtype=jnp.bfloat16),
            shape(depth, sources, dtype=jnp.bfloat16),
            shape(sources // lanes, lanes),
            shape(8, sources),
            shape(sources // lanes, lanes),
        ),
        (),
        cost,
    )(src, dst)

    lse = lax.all_to_all(lse, "col", 0, 0, tiled=True)
    src_potential, lse = call(
        target_kernel,
        (shape(sources // lanes, lanes), shape(rows, targets // lanes, lanes)),
        (),
        cost,
    )(lse, log_a, norms, row, share, a, b)

    lse = lax.all_to_all(lse, "row", 0, 0, tiled=True)
    new_potential = call(join_kernel, shape(targets // lanes, lanes))(lse, log_b, potential)
    return src_potential.reshape(sources), new_potential.reshape(targets)


def solution(mesh):
    return jax.shard_map(
        local,
        mesh=mesh,
        in_specs=(P(None, ("row", "col")), P(None, ("col", "row")), P("row"), P("col"), P("col")),
        out_specs=(P("row"), P("col")),
        check_vma=False,
    )
```

time: 173 us -> 172 us (level)
    pallas_call x1, Pallas kernels: 19.6 us -> 17.7 us  [local(): call(target_kernel, (shape(sources // lanes, lanes), shape(rows, targets...]
where the time goes in v4:
time: 172 us; the launch traced here: 171 us
  Pallas kernels  97.9 us (57%)
  blocking collectives  62.1 us (36%)
  starting transfers between devices  10.5 us (6%)
    pallas_call x1, Pallas kernels, local(): call(source_kernel, (shape(cols, sources // lanes, lanes), shape(targets,...  77.7 us
    all_gather x1, blocking collectives, local(): dst = lax.all_gather(dst, 'row')  26 us
    all_to_all x1, blocking collectives, local(): lse = lax.all_to_all(lse, 'col', 0, 0, tiled=True)  21.1 us
    pallas_call x1, Pallas kernels, local(): call(target_kernel, (shape(sources // lanes, lanes), shape(rows, targets...  17.7 us
    all_to_all x1, blocking collectives, local(): lse = lax.all_to_all(lse, 'row', 0, 0, tiled=True)  15 us
    all_to_all x1, starting transfers between devices, local(): src = lax.all_to_all(src, 'col', 0, 0, tiled=True)  10.5 us
  transfers between devices with their start and end apart: 1, of which 0 were waited for; matrix products, arithmetic and copies ran while one was open for 0% of the time, Pallas kernels for 0%

profile of v4, /device:TPU:1, one launch (start us, length us, event | category | flops | bytes accessed | tf_op | source)
XLA Modules:
  0.0 171.2 jit_solution(16246864748894376434)
XLA Ops:
  0.6 0.0 copy-start
  0.6 0.0 copy-start.1
  0.7 1.8 %shard_map.68 = (f32[32,32,128]{2,1,0:T(8,128)}, f32[80,128]{1,0:T(8,128)}) custom-call(f32[50,64]{1,0:T(8,128)} %src_hbm.1, f32[50,192]{1,0:T(8,128)} %dst_hbm.1, f32[16,128]{1,0:T(8,128)} %bitcast.11, f32[24,128]{1,0:T(8,128)} %bitcast.7), custom_call_target="tpu_custom_call" | custom-call | tf_op jit(solution)/shard_map/pallas_call | solution.py:323
  2.5 10.5 %all-to-all-start = ((f32[32,32,128]{2,1,0:T(8,128)}), f32[32,32,128]{2,1,0:T(8,128)S(1)}, u32[]{:S(2)}, u32[]{:S(2)}) async-start(f32[32,32,128]{2,1,0:T(8,128)} %get-tuple-element.13), calls=%async_computation | async-start | bytes 1048576 | tf_op jit(solution)/shard_map/all_to_all | solution.py:331
  13.0 26.0 %all-gather = f32[1280,128]{1,0:T(8,128)S(1)} all-gather(f32[80,128]{1,0:T(8,128)} %get-tuple-element.14), channel_id=2, replica_groups=mesh['row'=16,'col'=32] {'row'}, dimensions={0}, use_global_device_ids=true | all-gather | bytes 696320 | tf_op jit(solution)/shard_map/all_gather | solution.py:332
  39.0 0.0 all-to-all-done.src_ref
  39.0 77.7 %shard_map.69 = (f32[32,16,128]{2,1,0:T(8,128)S(1)}, f32[3072,2048]{1,0:T(8,128)S(1)}, bf16[3072,256]{1,0:T(8,128)(2,1)S(1)}, bf16[256,2048]{1,0:T(8,128)(2,1)S(...) custom-call(f32[32,32,128]{2,1,0:T(8,128)S(1)} %all-to-all-done.src_ref, ...), custom_call_target="tpu_custom_call" | custom-call | flops 3221225472 | bytes 5242880 | tf_op jit(solution)/shard_map/pallas_call | solution.py:334
  116.7 21.1 %all_to_all.15.lse_ref = f32[32,16,128]{2,1,0:T(8,128)S(1)} all-to-all(f32[32,16,128]{2,1,0:T(8,128)S(1)} %get-tuple-element.15), channel_id=1, replica_groups=mesh['row'=16,'col'=32] {'col'}, dimensions={0} | all-to-all | bytes 524288 | tf_op jit(solution)/shard_map/all_to_all | solution.py:349
  137.8 17.7 %shard_map.70 = (f32[16,128]{1,0:T(8,128)}, f32[16,24,128]{2,1,0:T(8,128)S(1)}) custom-call(f32[32,16,128]{2,1,0:T(8,128)S(1)} %all_to_all.15.lse_ref, f32[16,128]{1,0:T(8,128)S(1)} %get-tuple-element.16.log_a_ref, f32[16,128]{1,0:T(8,128)S(1)} %get-tuple-element.17.norm_ref, f32[8,2048]{1,0:T(8,128)S(1)} %get-tuple-element.18.row_ref, ...), custom_call_target="tpu_custom_call" | custom-call | flops 3221225472 | bytes 5242880 | tf_op jit(solution)/shard_map/pallas_call | solution.py:350
  155.5 15.0 %all_to_all.16.lse_ref = f32[16,24,128]{2,1,0:T(8,128)S(1)} all-to-all(f32[16,24,128]{2,1,0:T(8,128)S(1)} %get-tuple-element.23), channel_id=1, replica_groups=mesh['row'=16,'col'=32] {'row'}, dimensions={0} | all-to-all | bytes 393216 | tf_op jit(solution)/shard_map/all_to_all | solution.py:357
  170.5 0.0 copy-done
  170.5 0.0 copy-done.1
  170.5 0.7 shard_map.71
Async XLA Ops:
  0.6 169.8 %copy-start = (f32[3072]{0:T(1024)S(1)}, f32[3072]{0:T(1024)}, u32[]{:S(2)}) copy-start(f32[3072]{0:T(1024)} %param.9) | copy-start | bytes 36868
  0.6 169.8 %copy-start.1 = (f32[3072]{0:T(1024)S(1)}, f32[3072]{0:T(1024)}, u32[]{:S(2)}) copy-start(f32[3072]{0:T(1024)} %param.8) | copy-start | bytes 36868
  2.5 36.5 %all-to-all-start = ((f32[32,32,128]{2,1,0:T(8,128)}), f32[32,32,128]{2,1,0:T(8,128)S(1)}, u32[]{:S(2)}, u32[]{:S(2)}) async-start(f32[32,32,128]{2,1,0:T(8,128)} %get-tuple-element.13), calls=%async_computation | async-start | bytes 1048576 | tf_op jit(solution)/shard_map/all_to_all | solution.py:331

commit v5 on v4

--- a/solution.py
+++ b/solution.py
@@ -288,6 +288,10 @@
     )
 
 
+def listed_from(first, size):
+    return [[(first + k) % size for k in range(size)]]
+
+
 def shape(*dims, dtype=jnp.float32):
     return jax.ShapeDtypeStruct(dims, dtype)
 
@@ -346,7 +350,8 @@
         cost,
     )(src, dst)
 
-    lse = lax.all_to_all(lse, "col", 0, 0, tiled=True)
+    far = listed_from(cols // 2 + 2, cols)
+    lse = lax.all_to_all(lse, "col", 0, 0, axis_index_groups=far, tiled=True)
     src_potential, lse = call(
         target_kernel,
         (shape(sources // lanes, lanes), shape(rows, targets // lanes, lanes)),
@@ -354,7 +359,8 @@
         cost,
     )(lse, log_a, norms, row, share, a, b)
 
-    lse = lax.all_to_all(lse, "row", 0, 0, tiled=True)
+    quarter = listed_from(rows // 4, rows)
+    lse = lax.all_to_all(lse, "row", 0, 0, axis_index_groups=quarter, tiled=True)
     new_potential = call(join_kernel, shape(targets // lanes, lanes))(lse, log_b, potential)
     return src_potential.reshape(sources), new_potential.reshape(targets)
 

time: 172 us -> 166 us (0.965)
  blocking collectives: 62.1 us -> 56.2 us
    all_to_all x2, blocking collectives: 36.1 us -> 30.2 us  [the longest x1 17.3 us: local(): lse = lax.all_to_all(lse, 'col', 0, 0, axis_index_groups=far, tiled=True)]
where the time goes in v5:
time: 166 us; the launch traced here: 165 us
  Pallas kernels  97.9 us (59%)
  blocking collectives  56.2 us (34%)
  starting transfers between devices  10.5 us (6%)
    pallas_call x1, Pallas kernels, local(): call(source_kernel, (shape(cols, sources // lanes, lanes), shape(targets,...  77.7 us
    all_gather x1, blocking collectives, local(): dst = lax.all_gather(dst, 'row')  26 us
    pallas_call x1, Pallas kernels, local(): call(target_kernel, (shape(sources // lanes, lanes), shape(rows, targets...  17.7 us
    all_to_all x1, blocking collectives, local(): lse = lax.all_to_all(lse, 'col', 0, 0, axis_index_groups=far, tiled=True)  17.3 us
    all_to_all x1, blocking collectives, local(): lax.all_to_all(lse, 'row', 0, 0, axis_index_groups=quarter, tiled=True)  13 us
    all_to_all x1, starting transfers between devices, local(): src = lax.all_to_all(src, 'col', 0, 0, tiled=True)  10.5 us
  transfers between devices with their start and end apart: 1, of which 0 were waited for; matrix products, arithmetic and copies ran while one was open for 0% of the time, Pallas kernels for 0%

profile of v5, /device:TPU:1, one launch (start us, length us, event | category | flops | bytes accessed | tf_op | source)
XLA Modules:
  0.0 165.3 jit_solution(16432092624262002119)
XLA Ops:
  0.6 0.0 copy-start
  0.6 0.0 copy-start.1
  0.7 1.8 %shard_map.68 = (f32[32,32,128]{2,1,0:T(8,128)}, f32[80,128]{1,0:T(8,128)}) custom-call(f32[50,64]{1,0:T(8,128)} %src_hbm.1, f32[50,192]{1,0:T(8,128)} %dst_hbm.1, f32[16,128]{1,0:T(8,128)} %bitcast.11, f32[24,128]{1,0:T(8,128)} %bitcast.7), custom_call_target="tpu_custom_call" | custom-call | tf_op jit(solution)/shard_map/pallas_call | solution.py:327
  2.5 10.5 %all-to-all-start = ((f32[32,32,128]{2,1,0:T(8,128)}), f32[32,32,128]{2,1,0:T(8,128)S(1)}, u32[]{:S(2)}, u32[]{:S(2)}) async-start(f32[32,32,128]{2,1,0:T(8,128)} %get-tuple-element.13), calls=%async_computation | async-start | bytes 1048576 | tf_op jit(solution)/shard_map/all_to_all | solution.py:335
  13.0 26.0 %all-gather = f32[1280,128]{1,0:T(8,128)S(1)} all-gather(f32[80,128]{1,0:T(8,128)} %get-tuple-element.14), channel_id=2, replica_groups=mesh['row'=16,'col'=32] {'row'}, dimensions={0}, use_global_device_ids=true | all-gather | bytes 696320 | tf_op jit(solution)/shard_map/all_gather | solution.py:336
  39.0 0.0 all-to-all-done.src_ref
  39.0 77.7 %shard_map.69 = (f32[32,16,128]{2,1,0:T(8,128)S(1)}, f32[3072,2048]{1,0:T(8,128)S(1)}, bf16[3072,256]{1,0:T(8,128)(2,1)S(1)}, bf16[256,2048]{1,0:T(8,128)(2,1)S(...) custom-call(f32[32,32,128]{2,1,0:T(8,128)S(1)} %all-to-all-done.src_ref, ...), custom_call_target="tpu_custom_call" | custom-call | flops 3221225472 | bytes 5242880 | tf_op jit(solution)/shard_map/pallas_call | solution.py:338
  116.7 17.3 %all_to_all.15.lse_ref = f32[32,16,128]{2,1,0:T(8,128)S(1)} all-to-all(f32[32,16,128]{2,1,0:T(8,128)S(1)} %get-tuple-element.15), channel_id=1, replica_groups={{18,19,20,21,22,23,24,25,26,27,28,29,30,31,0,1,2,3,4,5,6,7,8,9,10,11,12..., dimensions={0} | all-to-all | bytes 524288 | tf_op jit(solution)/shard_map/all_to_all | solution.py:354
  133.9 17.7 %shard_map.70 = (f32[16,128]{1,0:T(8,128)}, f32[16,24,128]{2,1,0:T(8,128)S(1)}) custom-call(f32[32,16,128]{2,1,0:T(8,128)S(1)} %all_to_all.15.lse_ref, f32[16,128]{1,0:T(8,128)S(1)} %get-tuple-element.16.log_a_ref, f32[16,128]{1,0:T(8,128)S(1)} %get-tuple-element.17.norm_ref, f32[8,2048]{1,0:T(8,128)S(1)} %get-tuple-element.18.row_ref, ...), custom_call_target="tpu_custom_call" | custom-call | flops 3221225472 | bytes 5242880 | tf_op jit(solution)/shard_map/pallas_call | solution.py:355
  151.6 13.0 %all_to_all.16.lse_ref = f32[16,24,128]{2,1,0:T(8,128)S(1)} all-to-all(f32[16,24,128]{2,1,0:T(8,128)S(1)} %get-tuple-element.23), channel_id=1, replica_groups={{128,160,192,224,256,288,320,352,384,416,448,480,0,32,64,96},{129,161,1..., dimensions={0} | all-to-all | bytes 393216 | tf_op jit(solution)/shard_map/all_to_all | solution.py:363
  164.6 0.0 copy-done
  164.6 0.0 copy-done.1
  164.6 0.7 shard_map.71
Async XLA Ops:
  0.6 164.0 %copy-start = (f32[3072]{0:T(1024)S(1)}, f32[3072]{0:T(1024)}, u32[]{:S(2)}) copy-start(f32[3072]{0:T(1024)} %param.9) | copy-start | bytes 36868
  0.6 163.9 %copy-start.1 = (f32[3072]{0:T(1024)S(1)}, f32[3072]{0:T(1024)}, u32[]{:S(2)}) copy-start(f32[3072]{0:T(1024)} %param.8) | copy-start | bytes 36868
  2.5 36.5 %all-to-all-start = ((f32[32,32,128]{2,1,0:T(8,128)}), f32[32,32,128]{2,1,0:T(8,128)S(1)}, u32[]{:S(2)}, u32[]{:S(2)}) async-start(f32[32,32,128]{2,1,0:T(8,128)} %get-tuple-element.13), calls=%async_computation | async-start | bytes 1048576 | tf_op jit(solution)/shard_map/all_to_all | solution.py:335
